TPU v7x, 512 devices: a whole 4x8x8 slice. The times are simulated.
512 devices in a mesh: members: 8 (over y), bands: 64 (over z, x, core).
Axes of the slice: x: 4, y: 8, z: 8, core: 2. Of those that a mesh axis runs over, the one named last changes fastest.
Arguments:
- ensemble: float32 [128, 1024, 128], P('members', 'bands'), may hold values from -6 to 6
- neighbours: int32 [1024, 4], P('bands'), may hold values from 0 to 1023, as said below
- regime: int32 [1024], P('bands'), may hold values from 0 to 3
- norm_gain: float32 [128], replicated, may hold values from 0.25 to 1.75
- up_weight: bfloat16 [4, 128, 512], replicated, may hold values from -0.5 to 0.5
- down_weight: bfloat16 [4, 512, 128], replicated, may hold values from -0.25 to 0.25
- vertical_modes: float32 [4, 128], replicated, may hold values from -3 to 3
- obs_col: int32 [16384], P('bands'), may hold values from 0 to 1023, as said below
- obs_lev: int32 [16384], P('bands'), may hold values from 0 to 127
- obs_val: float32 [16384], P('bands'), may hold values from -9 to 9
- obs_err: float32 [16384], P('bands'), may hold values from 0.3 to 1
Outputs:
- analysis: float32 [128, 1024, 128], P('members', 'bands')
Inputs may be any that keep to these rules, and one draw needn't show every extreme that they name: `neighbours`: every neighbour of column c lies within 8 columns of c. `obs_col`: the observations at positions b * 256 to (b + 1) * 256 - 1 lie in columns b * 16 to (b + 1) * 16 - 1.
All inputs are finite; a program needn't handle non-finite values.
Results may differ from a plain program's by a relative error of at most 0.0034.
Values sent between devices are 32-bit elements; how exact they have to be, the bound alone decides.
No kernel may reach another device: no remote copies, remote signals or barrier semaphores. Data moves between devices by JAX's collectives and lax.ppermute only.
A program may use at most 64 MiB of HBM per device.

v0:
```python
import math
import jax
import jax.numpy as jnp
from jax import lax
from jax.sharding import PartitionSpec as P

E = 4
L = 4
NB = 4
HALO = 8
NS_ITERS = 4
highest = lax.Precision.HIGHEST


def extended(block, sides, width):
    for axis, dim in sides:
        count = lax.axis_size(axis)
        forward = [(i, i + 1) for i in range(count - 1)]
        backward = [(target, source) for source, target in forward]
        low = lax.ppermute(
            lax.slice_in_dim(block, block.shape[dim] - width, None, axis=dim), axis, forward
        )
        high = lax.ppermute(lax.slice_in_dim(block, 0, width, axis=dim), axis, backward)
        block = jnp.concatenate([low, block, high], axis=dim)
    return block


def analysis_coefficients(gram_matrix, cross_terms, drive_terms):
    order_k = gram_matrix.shape[0]
    identity = jnp.eye(order_k, dtype=jnp.float32)
    system = identity + gram_matrix
    norm_scale = jnp.sqrt(jnp.sum(system * system))
    iterate = system / norm_scale
    inverse = identity
    for sweep_index in range(NS_ITERS):
        if sweep_index == 0:
            product = iterate
        else:
            product = jnp.dot(inverse, iterate, precision=highest)
        factor = 1.5 * identity - 0.5 * product
        if sweep_index + 1 < NS_ITERS:
            iterate = jnp.dot(iterate, factor, precision=highest)
        if sweep_index == 0:
            inverse = factor
        else:
            inverse = jnp.dot(factor, inverse, precision=highest)
    root_factor = inverse / jnp.sqrt(norm_scale)
    weights_matrix = jnp.dot(root_factor, root_factor, precision=highest)
    mean_weights = jnp.dot(weights_matrix, drive_terms, precision=highest)
    return mean_weights[:, None] - 0.5 * jnp.dot(weights_matrix, cross_terms, precision=highest)


def per_device(
    ensemble,
    neighbours,
    regime,
    norm_gain,
    up_weight,
    down_weight,
    vertical_modes,
    obs_col,
    obs_lev,
    obs_val,
    obs_err,
):
    member_deviation, column_deviation, level_count = ensemble.shape
    band_index = lax.axis_index("bands")
    group_index = lax.axis_index("members")
    widened = extended(ensemble, (("bands", 1),), HALO)
    local_nb = neighbours - band_index * column_deviation + HALO
    summed_nb = jnp.zeros_like(ensemble)
    for which in range(NB):
        summed_nb = summed_nb + widened[:, local_nb[:, which], :]
    filtered_profile = ensemble + 0.5 * (0.25 * summed_nb - ensemble)
    flat = filtered_profile.reshape(member_deviation * column_deviation, level_count)
    inv_rms = lax.rsqrt(jnp.mean(flat * flat, axis=1, keepdims=True) + 1e-05)
    normed = (flat * inv_rms * norm_gain).astype(jnp.bfloat16)
    hidden = jax.nn.silu(
        jnp.einsum("rl,elf->erf", normed, up_weight, preferred_element_type=jnp.float32)
    ).astype(jnp.bfloat16)
    expert_out = jnp.einsum("erf,efl->erl", hidden, down_weight, preferred_element_type=jnp.float32)
    selected = regime[None, :] == jnp.arange(E, dtype=jnp.int32)[:, None]
    selected = jnp.tile(selected, (1, member_deviation))
    time_derivative = jnp.sum(jnp.where(selected[:, :, None], expert_out, 0.0), axis=0)
    predicted_vector = filtered_profile + time_derivative.reshape(
        member_deviation, column_deviation, level_count
    )
    vertical_lattice = lax.all_to_all(
        predicted_vector, "members", split_axis=1, concat_axis=0, tiled=True
    )
    share_cols = vertical_lattice.shape[1]
    average_sample_vector = jnp.mean(vertical_lattice, axis=0)
    sample_anomaly = vertical_lattice - average_sample_vector
    local_col = obs_col - band_index * column_deviation - group_index * share_cols
    inside = (local_col >= 0) & (local_col < share_cols)
    clipped = jnp.clip(local_col, 0, share_cols - 1)
    sampled = sample_anomaly[:, clipped, obs_lev]
    obs_pert = jnp.where(inside[None, :], sampled / obs_err, 0.0).T
    innovation = jnp.where(
        inside, (obs_val - average_sample_vector[clipped, obs_lev]) / obs_err, 0.0
    )
    members_all = obs_pert.shape[1]
    order_k = L * members_all
    obs_rows = obs_pert.shape[0]
    modulated = (vertical_modes[:, obs_lev].T[:, :, None] * obs_pert[:, None, :]).reshape(
        obs_rows, order_k
    ) / math.sqrt(order_k - 1)
    cross_part = jnp.dot(modulated.T, obs_pert, precision=highest)
    drive_part = jnp.dot(modulated.T, innovation, precision=highest)
    gram_part = jnp.dot(modulated.T, modulated, precision=highest)
    gram_matrix, cross_terms, drive_terms = lax.psum(
        (gram_part, cross_part, drive_part), ("members", "bands")
    )
    coefficients = analysis_coefficients(gram_matrix, cross_terms, drive_terms)
    coeff_modes = coefficients.reshape(L, members_all, members_all)
    update_correction = jnp.zeros_like(vertical_lattice)
    for layer in range(L):
        mixed = jnp.einsum("acv,ab->bcv", sample_anomaly, coeff_modes[layer], precision=highest)
        update_correction = update_correction + vertical_modes[layer][None, None, :] * mixed
    analysed = vertical_lattice + update_correction / math.sqrt(order_k - 1)
    return lax.all_to_all(analysed, "members", split_axis=0, concat_axis=1, tiled=True)


def solution(mesh):
    in_specs = (
        P("members", "bands", None),
        P("bands", None),
        P("bands"),
        P(),
        P(),
        P(),
        P(),
        P("bands"),
        P("bands"),
        P("bands"),
        P("bands"),
    )
    out_specs = P("members", "bands", None)
    return jax.shard_map(
        per_device, mesh=mesh, in_specs=in_specs, out_specs=out_specs, check_vma=False
    )
```

profile of v0, /device:TPU:8, one launch (start us, length us, event | category | flops | bytes accessed | tf_op | source)
XLA Modules:
  0.0 368.7 jit_solution(5785162211855150360)
XLA Ops:
  6.5 0.9 fusion.62
  7.5 1.9 collective-permute-start
  9.4 1.3 collective-permute-start.1
  10.7 0.7 iota_compare_fusion.4
  11.4 0.7 subtract_add_fusion
  12.2 0.8 copy.73
  13.0 0.9 constant_dynamic-update-slice_fusion.1
  14.0 0.6 gather_fusion.3
  14.6 0.6 gather_fusion.2
  15.2 0.6 gather_fusion.1
  15.7 0.6 gather_fusion
  16.3 0.1 multiply_reduce_fusion.1
  16.7 0.1 fusion.35
  16.9 1.0 fusion.6
  17.9 0.7 copy_add_fusion
  18.6 8.6 %all-to-all-start = ((f32[16,16,128]{2,0,1:T(8,128)}), f32[16,16,128]{2,0,1:T(8,128)S(1)}, u32[]{:S(2)}, u32[]{:S(2)}) async-start(f32[16,16,128]{2,0,1:T(8,128)} %copy_add_fusion), calls=%async_computation | async-start | bytes 262144 | tf_op jit(solution)/shard_map/all_to_all | solution.py:88
  27.3 0.7 gather_fusion.4
  28.0 8.0 %all-to-all-done = f32[16,16,128]{2,0,1:T(8,128)S(1)} async-done(((f32[16,16,128]{2,0,1:T(8,128)}), f32[16,16,128]{2,0,1:T(8,128)S(1)}, u32[]{:S(2)}, u32[]{:S(2)}) %all-to-all-start) | async-done | bytes 131104 | tf_op jit(solution)/shard_map/all_to_all | solution.py:88
  36.1 2.4 gather_fusion.6
  38.6 1.9 gather_fusion.5
  40.6 0.1 divide_select_fusion
  40.7 0.3 multiply_multiply_fusion
  41.1 1.7 fusion.17
  42.8 2.1 fusion.19
  44.9 0.7 copy-done.4
  45.5 0.4 fusion.21
  45.9 104.2 %psum.22 = f32[512]{0:T(512)S(1)} all-reduce(f32[512]{0:T(512)S(1)} %bitcast.136), channel_id=1, replica_groups=mesh['members'=8,'bands'=64] {'members','bands'}, use_global_device_ids=true, to_apply=%region_5.6 | all-reduce | flops 512 | bytes 4096 | tf_op jit(solution)/shard_map/psum | solution.py:111
  150.2 169.8 %all-reduce.3.cloned.1.call-done = (f32[512,512]{1,0:T(8,128)}, f32[512,128]{1,0:T(8,128)}) async-done(((f32[512,512]{1,0:T(8,128)}, f32[512,128]{1,0:T(8,128)}), (f32[512,512]{1,0:T(8,128)}, f32[512,128]{1,0:T(8,128)})) %all-reduce.3.cloned.1.call-update) | async-done | bytes 1310736 | tf_op jit(solution)/shard_map/psum | solution.py:111
  320.0 2.2 multiply_reduce_fusion
  322.9 2.0 fusion.14
  324.9 2.0 select_subtract_fusion.2
  326.9 2.0 fusion.13
  328.9 1.8 fusion.63
  330.8 1.9 select_subtract_fusion.1
  332.6 1.8 fusion.64
  334.5 2.1 fusion.65
  336.6 1.8 select_subtract_fusion
  338.4 1.8 convolution_divide_fusion
  340.3 1.8 fusion.66
  342.1 1.0 fusion.67
  343.1 1.0 fusion.7
  344.1 0.3 convolution_multiply_fusion.4
  344.5 0.3 convolution_multiply_fusion.5
  344.8 0.3 convolution_multiply_fusion.6
  345.1 0.3 fusion.12
  345.4 0.1 copy.79
  345.5 15.6 %all_to_all.36 = f32[128,2,128]{2,1,0:T(2,128)S(1)} all-to-all(f32[128,2,128]{2,1,0:T(2,128)S(1)} %copy.79), channel_id=1, replica_groups=mesh['members'=8,'bands'=64] {'members'}, dimensions={0} | all-to-all | bytes 262144 | tf_op jit(solution)/shard_map/all_to_all | solution.py:121
  361.2 0.7 copy.80
  (48 shorter events, 0.7 us)
Async XLA Ops:
  6.5 10.3 %copy-start = (bf16[4,512,128]{2,1,0:T(8,128)(2,1)S(1)}, bf16[4,512,128]{2,1,0:T(8,128)(2,1)}, u32[]{:S(2)}) copy-start(bf16[4,512,128]{2,1,0:T(8,128)(2,1)} %param.16) | copy-start | bytes 1572868
  7.5 8.8 %copy-start.1 = (f32[16,16,128]{2,1,0:T(8,128)S(1)}, f32[16,16,128]{2,1,0:T(8,128)}, u32[]{:S(2)}) copy-start(f32[16,16,128]{2,1,0:T(8,128)} %param.11) | copy-start | bytes 393220
  7.5 5.5 %collective-permute-start = (f32[16,8,128]{2,0,1:T(8,128)S(1)}, f32[16,8,128]{2,0,1:T(8,128)S(1)}, u32[]{:S(2)}, u32[]{:S(2)}) collective-permute-start(f32[16,8,128]{2,0,1:T(8,128)S(1)} %copy.107), channel_id=1, source_target_pairs={{0,1},{1,2},{2,3},{3,4},{4,5},{5,6},{6,7},{7,8},{8,9},{9,10},{10,1... | collective-permute-start | bytes 196616 | tf_op jit(solution)/shard_map/ppermute | solution.py:20
  9.4 4.6 %collective-permute-start.1 = (f32[16,8,128]{2,0,1:T(8,128)S(1)}, f32[16,8,128]{2,0,1:T(8,128)S(1)}, u32[]{:S(2)}, u32[]{:S(2)}) collective-permute-start(f32[16,8,128]{2,0,1:T(8,128)S(1)} %copy.108), channel_id=1, source_target_pairs={{1,0},{2,1},{3,2},{4,3},{5,4},{6,5},{7,6},{8,7},{9,8},{10,9},{11,1... | collective-permute-start | bytes 196616 | tf_op jit(solution)/shard_map/ppermute | solution.py:23
  14.0 2.7 copy-start.9
  14.6 2.2 copy-start.10
  16.8 10.4 %copy-start.6 = (s32[256]{0:T(256)S(1)}, s32[256]{0:T(256)}, u32[]{:S(2)}) copy-start(s32[256]{0:T(256)} %param.18) | copy-start | bytes 3076
  16.8 10.4 %copy-start.7 = (s32[256]{0:T(256)S(1)}, s32[256]{0:T(256)}, u32[]{:S(2)}) copy-start(s32[256]{0:T(256)} %param.19) | copy-start | bytes 3076
  18.6 17.4 %all-to-all-start = ((f32[16,16,128]{2,0,1:T(8,128)}), f32[16,16,128]{2,0,1:T(8,128)S(1)}, u32[]{:S(2)}, u32[]{:S(2)}) async-start(f32[16,16,128]{2,0,1:T(8,128)} %copy_add_fusion), calls=%async_computation | async-start | bytes 262144 | tf_op jit(solution)/shard_map/all_to_all | solution.py:88
  27.2 292.8 %all-reduce.3.cloned.1.call-start = ((), (), s32[]{:S(2)}) async-start(), calls=%async_computation.2 | async-start | bytes 2621440 | tf_op jit(solution)/shard_map/psum | solution.py:111
  38.5 2.1 copy-start.5
  38.5 2.1 copy-start.8
  44.8 0.7 copy-start.4
  320.0 2.9 copy-start.2
  342.1 1.0 copy-start.3
Sparse Core Ops, SparseCore 0:
  45.0 274.9 all-reduce.2
where the time goes:
time: 369 us
  waiting for transfers between devices  178 us (48%)
  blocking collectives  120 us (33%)
  matrix products  27.5 us (7%)
  between operations  14.6 us (4%)
  local copies, waits for them, and re-layouts  11.9 us (3%)
  starting transfers between devices  11.8 us (3%)
  other arithmetic  5.08 us (1%)
    psum x1, waiting for transfers between devices, per_device(): lax.psum((gram_part, cross_part, drive_part), ('members', 'bands'))  170 us
    psum x1, blocking collectives, per_device(): lax.psum((gram_part, cross_part, drive_part), ('members', 'bands'))  104 us
    all_to_all x1, blocking collectives, per_device(): lax.all_to_all(analysed, 'members', split_axis=0, concat_axis=1, tiled=True)  15.6 us
    all_to_all x1, starting transfers between devices, per_device(): lax.all_to_all(predicted_vector, 'members', split_axis=1, concat_axis=0,...  8.65 us
    all_to_all x1, waiting for transfers between devices, per_device(): lax.all_to_all(predicted_vector, 'members', split_axis=1, concat_axis=0,...  7.98 us
  transfers between devices with their start and end apart: 4, of which 2 were waited for; matrix products, arithmetic and copies ran while one was open for 1% of the time, Pallas kernels for 0%

commit v1 on v0

--- a/solution.py
+++ b/solution.py
@@ -108,9 +108,13 @@
     cross_part = jnp.dot(modulated.T, obs_pert, precision=highest)
     drive_part = jnp.dot(modulated.T, innovation, precision=highest)
     gram_part = jnp.dot(modulated.T, modulated, precision=highest)
-    gram_matrix, cross_terms, drive_terms = lax.psum(
-        (gram_part, cross_part, drive_part), ("members", "bands")
-    )
+
+    def _link_regions(sample):
+        for j in ("bands", "members"):
+            sample = lax.psum(sample, j)
+        return sample
+
+    gram_matrix, cross_terms, drive_terms = _link_regions((gram_part, cross_part, drive_part))
     coefficients = analysis_coefficients(gram_matrix, cross_terms, drive_terms)
     coeff_modes = coefficients.reshape(L, members_all, members_all)
     update_correction = jnp.zeros_like(vertical_lattice)

time: 369 us -> 436 us (1.18)
  blocking collectives: 120 us -> 156 us
  waiting for transfers between devices: 178 us -> 209 us
    psum x1 -> x2, blocking collectives: 104 us -> 142 us  [_link_regions(): sample = lax.psum(sample, j)]
    psum x1 -> x2, waiting for transfers between devices: 170 us -> 201 us  [_link_regions(): sample = lax.psum(sample, j)]
  transfers between devices with their start and end apart: 4 -> 5, of which waited for: 2 -> 2; matrix products, arithmetic and copies ran while one was open for 1% -> 1% of each run, Pallas kernels for 0% -> 0%
where the time goes in v1:
time: 436 us; the launch traced here: 435 us
  waiting for transfers between devices  209 us (48%)
  blocking collectives  156 us (36%)
  matrix products  27.5 us (6%)
  between operations  14.7 us (3%)
  starting transfers between devices  11.9 us (3%)
  local copies, waits for them, and re-layouts  11.3 us (3%)
  other arithmetic  5.08 us (1%)
    psum x2, waiting for transfers between devices, _link_regions(): sample = lax.psum(sample, j)  201 us
    psum x2, blocking collectives, _link_regions(): sample = lax.psum(sample, j)  142 us
    all_to_all x1, blocking collectives, per_device(): lax.all_to_all(analysed, 'members', split_axis=0, concat_axis=1, tiled=True)  13.7 us
  transfers between devices with their start and end apart: 5, of which 2 were waited for; matrix products, arithmetic and copies ran while one was open for 1% of the time, Pallas kernels for 0%

profile of v1, /device:TPU:8, one launch (start us, length us, event | category | flops | bytes accessed | tf_op | source)
XLA Modules:
  0.0 435.4 jit_solution(16870338438022388290)
XLA Ops:
  6.5 0.9 fusion.62
  7.5 1.9 collective-permute-start
  9.4 1.3 collective-permute-start.1
  10.7 0.7 iota_compare_fusion.4
  11.4 0.7 subtract_add_fusion
  12.2 0.8 copy.73
  13.0 0.9 constant_dynamic-update-slice_fusion.1
  14.0 0.6 gather_fusion.3
  14.6 0.6 gather_fusion.2
  15.2 0.6 gather_fusion.1
  15.7 0.6 gather_fusion
  16.3 0.1 multiply_reduce_fusion.1
  16.7 0.1 fusion.35
  16.9 1.0 fusion.6
  17.9 0.7 copy_add_fusion
  18.6 8.6 %all-to-all-start = ((f32[16,16,128]{2,0,1:T(8,128)}), f32[16,16,128]{2,0,1:T(8,128)S(1)}, u32[]{:S(2)}, u32[]{:S(2)}) async-start(f32[16,16,128]{2,0,1:T(8,128)} %copy_add_fusion), calls=%async_computation | async-start | bytes 262144 | tf_op jit(solution)/shard_map/all_to_all | solution.py:88
  27.3 0.7 gather_fusion.4
  28.0 8.0 %all-to-all-done = f32[16,16,128]{2,0,1:T(8,128)S(1)} async-done(((f32[16,16,128]{2,0,1:T(8,128)}), f32[16,16,128]{2,0,1:T(8,128)S(1)}, u32[]{:S(2)}, u32[]{:S(2)}) %all-to-all-start) | async-done | bytes 131104 | tf_op jit(solution)/shard_map/all_to_all | solution.py:88
  36.1 2.4 gather_fusion.6
  38.6 1.9 gather_fusion.5
  40.6 0.1 divide_select_fusion
  40.7 0.3 multiply_multiply_fusion
  41.1 1.7 fusion.17
  42.7 2.1 fusion.19
  44.9 200.9 %all-reduce.5.cloned.1.call-done = (f32[512,512]{1,0:T(8,128)}, f32[512,128]{1,0:T(8,128)}) async-done(((f32[512,512]{1,0:T(8,128)}, f32[512,128]{1,0:T(8,128)}), (f32[512,512]{1,0:T(8,128)}, f32[512,128]{1,0:T(8,128)})) %all-reduce.5.cloned.1.call-update) | async-done | bytes 1310736 | tf_op jit(solution)/shard_map/psum | solution.py:114
  245.9 0.4 fusion.21
  246.3 126.5 %psum.44 = f32[512]{0:T(512)S(1)} all-reduce(f32[512]{0:T(512)S(1)} %bitcast.136), channel_id=1, replica_groups=mesh['members'=8,'bands'=64] {'bands'}, use_global_device_ids=true, to_apply=%region_6.7 | all-reduce | flops 512 | bytes 4096 | tf_op jit(solution)/shard_map/psum | solution.py:114
  372.8 15.9 %psum.45 = f32[512]{0:T(512)S(1)} all-reduce(f32[512]{0:T(512)S(1)} %psum.44), channel_id=1, replica_groups=mesh['members'=8,'bands'=64] {'members'}, use_global_device_ids=true, to_apply=%region_7.8 | all-reduce | flops 512 | bytes 4096 | tf_op jit(solution)/shard_map/psum | solution.py:114
  388.7 2.2 multiply_reduce_fusion
  391.6 2.0 fusion.14
  393.6 2.0 select_subtract_fusion.2
  395.6 2.0 fusion.13
  397.6 1.8 fusion.63
  399.4 1.9 select_subtract_fusion.1
  401.3 1.8 fusion.64
  403.1 2.1 fusion.65
  405.2 1.8 select_subtract_fusion
  407.1 1.9 convolution_divide_fusion
  409.0 1.8 fusion.66
  410.8 1.0 fusion.67
  411.8 1.0 fusion.7
  412.8 0.3 convolution_multiply_fusion.4
  413.1 0.3 convolution_multiply_fusion.5
  413.5 0.3 convolution_multiply_fusion.6
  413.8 0.3 fusion.12
  414.1 0.1 copy.79
  414.2 13.7 %all_to_all.36 = f32[128,2,128]{2,1,0:T(2,128)S(1)} all-to-all(f32[128,2,128]{2,1,0:T(2,128)S(1)} %copy.79), channel_id=1, replica_groups=mesh['members'=8,'bands'=64] {'members'}, dimensions={0} | all-to-all | bytes 262144 | tf_op jit(solution)/shard_map/all_to_all | solution.py:125
  427.9 0.7 copy.80
  (52 shorter events, 0.7 us)
Async XLA Ops:
  6.5 10.3 %copy-start = (bf16[4,512,128]{2,1,0:T(8,128)(2,1)S(1)}, bf16[4,512,128]{2,1,0:T(8,128)(2,1)}, u32[]{:S(2)}) copy-start(bf16[4,512,128]{2,1,0:T(8,128)(2,1)} %param.16) | copy-start | bytes 1572868
  7.5 8.8 %copy-start.1 = (f32[16,16,128]{2,1,0:T(8,128)S(1)}, f32[16,16,128]{2,1,0:T(8,128)}, u32[]{:S(2)}) copy-start(f32[16,16,128]{2,1,0:T(8,128)} %param.11) | copy-start | bytes 393220
  7.5 5.5 %collective-permute-start = (f32[16,8,128]{2,0,1:T(8,128)S(1)}, f32[16,8,128]{2,0,1:T(8,128)S(1)}, u32[]{:S(2)}, u32[]{:S(2)}) collective-permute-start(f32[16,8,128]{2,0,1:T(8,128)S(1)} %copy.107), channel_id=1, source_target_pairs={{0,1},{1,2},{2,3},{3,4},{4,5},{5,6},{6,7},{7,8},{8,9},{9,10},{10,1... | collective-permute-start | bytes 196616 | tf_op jit(solution)/shard_map/ppermute | solution.py:20
  9.4 4.6 %collective-permute-start.1 = (f32[16,8,128]{2,0,1:T(8,128)S(1)}, f32[16,8,128]{2,0,1:T(8,128)S(1)}, u32[]{:S(2)}, u32[]{:S(2)}) collective-permute-start(f32[16,8,128]{2,0,1:T(8,128)S(1)} %copy.108), channel_id=1, source_target_pairs={{1,0},{2,1},{3,2},{4,3},{5,4},{6,5},{7,6},{8,7},{9,8},{10,9},{11,1... | collective-permute-start | bytes 196616 | tf_op jit(solution)/shard_map/ppermute | solution.py:23
  14.0 2.7 copy-start.9
  14.6 2.2 copy-start.10
  16.8 10.4 %copy-start.6 = (s32[256]{0:T(256)S(1)}, s32[256]{0:T(256)}, u32[]{:S(2)}) copy-start(s32[256]{0:T(256)} %param.18) | copy-start | bytes 3076
  16.8 10.4 %copy-start.7 = (s32[256]{0:T(256)S(1)}, s32[256]{0:T(256)}, u32[]{:S(2)}) copy-start(s32[256]{0:T(256)} %param.19) | copy-start | bytes 3076
  18.6 17.4 %all-to-all-start = ((f32[16,16,128]{2,0,1:T(8,128)}), f32[16,16,128]{2,0,1:T(8,128)S(1)}, u32[]{:S(2)}, u32[]{:S(2)}) async-start(f32[16,16,128]{2,0,1:T(8,128)} %copy_add_fusion), calls=%async_computation | async-start | bytes 262144 | tf_op jit(solution)/shard_map/all_to_all | solution.py:88
  27.2 218.6 %all-reduce.5.cloned.1.call-start = ((), (), s32[]{:S(2)}) async-start(), calls=%async_computation.2 | async-start | bytes 2621440 | tf_op jit(solution)/shard_map/psum | solution.py:114
  38.5 2.1 copy-start.5
  38.5 2.1 copy-start.8
  44.8 201.0 %copy-start.4 = (f32[4,128]{1,0:T(4,128)S(1)}, f32[4,128]{1,0:T(4,128)}, u32[]{:S(2)}) copy-start(f32[4,128]{1,0:T(4,128)} %param.17) | copy-start | bytes 6148
  44.8 343.8 %all-reduce.7.cloned.1.call-start = ((), (), s32[]{:S(2)}) async-start(), calls=%async_computation.3 | async-start | bytes 2621440 | tf_op jit(solution)/shard_map/psum | solution.py:114
  388.7 2.9 copy-start.2
  410.8 1.0 copy-start.3
Sparse Core Ops, SparseCore 0:
  45.0 200.8 all-reduce.4
  248.4 80.0 all-reduce.6
